TPU v7x, 256 devices: a whole 4x4x8 slice. The times are simulated.
256 devices in a mesh: dst: 32 (over x, z), src: 8 (over y, core).
Axes of the slice: x: 4, y: 4, z: 8, core: 2. Of those that a mesh axis runs over, the one named last changes fastest.
Arguments:
- node_feats: bfloat16 [8, 32, 256, 128], P('src', 'dst'), may hold values from -16 to 16
- w_query: bfloat16 [128, 128], replicated, may hold values from -1 to 1
- w_key: bfloat16 [128, 128], replicated, may hold values from -1 to 1
- w_value: bfloat16 [128, 128], replicated, may hold values from -0.5 to 0.5
- w_out: bfloat16 [128, 128], replicated, may hold values from -0.5 to 0.5
- src_blocks: int32 [8, 32, 16, 16], P('src', 'dst'), may hold values from 0 to 63, as said below
- live_counts: int32 [8, 32, 16], P('src', 'dst'), may hold values from 1 to 16, as said below
- edge_bits: int32 [8, 32, 16, 16, 16, 128], P('src', 'dst'), may hold values from 0 to 255, as said below
Outputs:
- mixed_rows: bfloat16 [8, 32, 256, 128], P('src', 'dst')
Inputs may be any that keep to these rules, and one draw needn't show every extreme that they name: `src_blocks`: each list holds 16 different source block numbers of its source group. Entries from live_counts onward in a list are unused; 16 is reached in every draw. `edge_bits`: in list entry 0 every row t links to column t.
All inputs are finite; a program needn't handle non-finite values.
Results may differ from a plain program's by a relative error of at most 0.015.
Values may be sent and summed in bfloat16 or wider, within the bound.
No kernel may reach another device: no remote copies, remote signals or barrier semaphores. Data moves between devices by JAX's collectives and lax.ppermute only.
A program may use at most 64 MiB of HBM per device.

v0:
```python
import math

import jax
import jax.numpy as jnp
from jax import lax
from jax.sharding import PartitionSpec as P

HEADS = 4
BLK = 128


def unpack_links(slot_words):
    bit_shifts = jnp.arange(8, dtype=jnp.int32)
    bit_values = jnp.bitwise_and(
        jnp.right_shift(slot_words[:, :, None, :], bit_shifts[None, None, :, None]), 1
    )
    return bit_values.reshape(slot_words.shape[0], -1, slot_words.shape[2]) == 1


def shards(node_feats, w_query, w_key, w_value, w_out, src_blocks, live_counts, edge_bits):
    own_rows = node_feats[0, 0]
    row_count, model_width = own_rows.shape
    head_dim = model_width // HEADS
    per_group = row_count // BLK
    own_queries = jnp.dot(own_rows, w_query, preferred_element_type=jnp.float32).astype(
        jnp.bfloat16
    )
    dest_queries = lax.all_gather(own_queries, "src", axis=0, tiled=True)
    w_pair = jnp.concatenate([w_key, w_value], axis=1)
    own_pairs = jnp.dot(own_rows, w_pair, preferred_element_type=jnp.float32).astype(jnp.bfloat16)
    source_pairs = lax.all_gather(own_pairs, "dst", axis=0, tiled=True)
    block_lists = src_blocks[0, 0]
    block_counts = live_counts[0, 0]
    block_words = edge_bits[0, 0]
    dest_count, slot_total = block_lists.shape
    group_count = dest_count // per_group
    query_blocks = dest_queries.reshape(dest_count, BLK, HEADS, head_dim)
    pair_blocks = source_pairs.reshape(-1, BLK, 2 * model_width)
    scale_factor = 1.0 / math.sqrt(head_dim)

    def visit_slot(slot_index, state_now):
        run_max, run_sum, run_acc = state_now
        picked = jnp.take(pair_blocks, block_lists[:, slot_index], axis=0)
        keys_here = picked[:, :, :model_width].reshape(dest_count, BLK, HEADS, head_dim)
        values_here = picked[:, :, model_width:].reshape(dest_count, BLK, HEADS, head_dim)
        scores = (
            jnp.einsum(
                "bchd,bthd->bhct", keys_here, query_blocks, preferred_element_type=jnp.float32
            )
            * scale_factor
        )
        slot_words = lax.dynamic_index_in_dim(block_words, slot_index, 1, keepdims=False)
        linked = unpack_links(slot_words) & (slot_index < block_counts)[:, None, None]
        linked = linked[:, None]
        new_max = jnp.maximum(run_max, jnp.max(jnp.where(linked, scores, -1e30), axis=2))
        weights = jnp.where(linked, jnp.exp(scores - new_max[:, :, None, :]), 0.0)
        factor = jnp.exp(run_max - new_max)
        new_sum = run_sum * factor + jnp.sum(weights, axis=2)
        added_part = jnp.einsum(
            "bhct,bchd->bthd",
            weights.astype(jnp.bfloat16),
            values_here,
            preferred_element_type=jnp.float32,
        )
        kept_part = (
            run_acc.reshape(dest_count, BLK, HEADS, head_dim)
            * jnp.transpose(factor, (0, 2, 1))[..., None]
        )
        new_acc = (kept_part + added_part).reshape(dest_count, BLK, model_width)
        return (new_max, new_sum, new_acc)

    initial = (
        jnp.full((dest_count, HEADS, BLK), -1e30, jnp.float32),
        jnp.zeros((dest_count, HEADS, BLK), jnp.float32),
        jnp.zeros((dest_count, BLK, model_width), jnp.float32),
    )
    run_max, run_sum, run_acc = lax.fori_loop(0, slot_total, visit_slot, initial)
    group_out = (
        run_acc.reshape(dest_count, BLK, HEADS, head_dim)
        / jnp.transpose(run_sum, (0, 2, 1))[..., None]
    )
    group_out = group_out.astype(jnp.bfloat16)
    maxima = run_max.reshape(group_count, per_group, HEADS, BLK)
    totals = run_sum.reshape(group_count, per_group, HEADS, BLK)
    outputs = group_out.reshape(group_count, per_group, BLK, HEADS, head_dim)
    row_peak = lax.pmax(maxima, "src")
    mass = totals * jnp.exp(maxima - row_peak)
    scaled_out = (
        outputs.astype(jnp.float32) * jnp.transpose(mass, (0, 1, 3, 2))[..., None]
    ).reshape(group_count, row_count, model_width)
    summed_den, summed_num = (
        lax.psum_scatter(mass, "src", scatter_dimension=0, tiled=True),
        lax.psum_scatter(scaled_out, "src", scatter_dimension=0, tiled=True),
    )
    denominator = summed_den[0]
    numerator = summed_num[0]
    denom_rows = jnp.transpose(denominator, (0, 2, 1)).reshape(row_count, HEADS)
    attended = (
        (numerator.reshape(row_count, HEADS, head_dim) / denom_rows[..., None])
        .reshape(row_count, model_width)
        .astype(jnp.bfloat16)
    )
    mixed_rows = jnp.dot(attended, w_out, preferred_element_type=jnp.float32).astype(jnp.bfloat16)
    return mixed_rows.reshape(1, 1, row_count, model_width)


def solution(mesh):
    in_specs = (
        P("src", "dst", None, None),
        P(),
        P(),
        P(),
        P(),
        P("src", "dst", None, None),
        P("src", "dst", None),
        P("src", "dst", None, None, None, None),
    )
    out_specs = P("src", "dst", None, None)
    return jax.shard_map(shards, mesh=mesh, in_specs=in_specs, out_specs=out_specs, check_vma=False)
```

profile of v0, /device:TPU:96, one launch (start us, length us, event | category | flops | bytes accessed | tf_op | source)
XLA Modules:
  0.0 408.3 jit_solution(2036607239307549865)
XLA Ops:
  9.1 3.2 copy.46
  12.5 13.6 %all_gather.7 = bf16[2048,128]{1,0:T(8,128)(2,1)S(1)} all-gather(bf16[256,128]{1,0:T(8,128)(2,1)S(1)} %convolution_convert_fusion.2), channel_id=1, replica_groups=mesh['dst'=32,'src'=8] {'src'}, dimensions={0}, use_global_device_ids=true | all-gather | bytes 589824 | tf_op jit(solution)/shard_map/all_gather | solution.py:28
  26.6 67.3 %all-gather.2.cloned.1.call-done = bf16[8192,256]{0,1:T(8,128)(2,1)} async-done(((bf16[256,256]{0,1:T(8,128)(2,1)}), bf16[8192,256]{0,1:T(8,128)(2,1)}) %all-gather.2.cloned.1.call-update) | async-done | bytes 4194320 | tf_op jit(solution)/shard_map/all_gather | solution.py:31
  94.0 6.4 %copy.43 = bf16[8192,256]{1,0:T(8,128)(2,1)} copy(bf16[8192,256]{0,1:T(8,128)(2,1)} %all-gather.2.cloned.1.call-done) | data formatting | bytes 8388608
  100.4 234.5 %while.18 = (s32[]{:T(128)}, f32[16,4,128]{2,1,0:T(4,128)S(1)}, f32[16,4,128]{2,1,0:T(4,128)S(1)}, f32[16,128,128]{1,2,0:T(8,128)S(1)}, s32[16,16,16,128]{3,2,0,...) while((s32[]{:T(128)}, f32[16,4,128]{2,1,0:T(4,128)S(1)}, ...), condition=%wide.region_3.4_spmd.clone, body=%wide.region_0.3_spmd.clone.sunk | while | flops 147899504 | bytes 26614284 | solution.py:77
  108.4 3.3 fusion.55
  123.0 3.3 fusion.55
  137.7 3.3 fusion.55
  152.4 3.3 fusion.55
  167.0 3.3 fusion.55
  181.7 3.3 fusion.55
  196.3 3.3 fusion.55
  211.0 3.3 fusion.55
  225.6 3.3 fusion.55
  240.3 3.3 fusion.55
  255.0 3.3 fusion.55
  269.6 3.3 fusion.55
  284.3 3.3 fusion.55
  298.9 3.3 fusion.55
  313.6 3.3 fusion.55
  328.3 3.3 fusion.55
  335.0 23.6 %pmax.7 = f32[8,2,4,128]{3,2,1,0:T(4,128)S(1)} all-reduce(f32[8,2,4,128]{3,2,1,0:T(4,128)S(1)} %bitcast.113), channel_id=1, replica_groups=mesh['dst'=32,'src'=8] {'src'}, use_global_device_ids=true, to_apply=%region_4.5 | all-reduce | flops 8192 | bytes 65536 | tf_op jit(solution)/shard_map/pmax | solution.py:86
  366.9 23.6 %all-reduce = f32[8,2,4,128]{3,2,1,0:T(4,128)S(1)} all-reduce(f32[8,2,4,128]{3,2,1,0:T(4,128)S(1)} %bitcast.123), channel_id=3, replica_groups=mesh['dst'=32,'src'=8] {'src'}, use_global_device_ids=true, to_apply=%region_6.7.clone | all-reduce | flops 8192 | bytes 65536
  391.3 8.5 %reduce-scatter.2.cloned.1.call-done = f32[1,256,128]{2,1,0:T(8,128)} async-done(((f32[8,256,128]{2,1,0:T(8,128)}), f32[1,256,128]{2,1,0:T(8,128)}) %reduce-scatter.2.cloned.1.call-update) | async-done | bytes 131088 | tf_op jit(solution)/shard_map/reduce_scatter | solution.py:93
  (315 shorter events, 195.2 us)
Async XLA Ops:
  6.5 0.8 copy-start
  6.5 5.7 %copy-start.3 = (s32[1,1,16,16]{3,2,1,0:T(8,128)S(1)}, s32[1,1,16,16]{3,2,1,0:T(8,128)}, u32[]{:S(2)}) copy-start(s32[1,1,16,16]{3,2,1,0:T(8,128)} %param.15) | copy-start | bytes 3076
  6.5 5.8 %copy-start.2 = (bf16[128,128]{1,0:T(8,128)(2,1)S(1)}, bf16[128,128]{1,0:T(8,128)(2,1)}, u32[]{:S(2)}) copy-start(bf16[128,128]{1,0:T(8,128)(2,1)} %param.11) | copy-start | bytes 98308
  6.5 87.4 %all-gather.2.cloned.1.call-start = ((), (), s32[]{:S(2)}) async-start(), calls=%async_computation.1 | async-start | bytes 4325376 | tf_op jit(solution)/shard_map/all_gather | solution.py:31
  9.0 390.7 %reduce-scatter.2.cloned.1.call-start = ((), (), s32[]{:S(2)}) async-start(), calls=%async_computation.2 | async-start | bytes 1179648 | tf_op jit(solution)/shard_map/reduce_scatter | solution.py:93
  26.6 73.8 %copy-start.5 = (s32[1,1,16]{2,1,0:T(1,128)S(1)}, s32[1,1,16]{2,1,0:T(1,128)}, u32[]{:S(2)}) copy-start(s32[1,1,16]{2,1,0:T(1,128)} %param.16) | copy-start | bytes 196
  362.2 1.7 copy-start.1
  363.6 2.8 copy-start.6
  363.6 36.2 %copy-start.4 = (bf16[128,128]{1,0:T(8,128)(2,1)S(1)}, bf16[128,128]{1,0:T(8,128)(2,1)}, u32[]{:S(2)}) copy-start(bf16[128,128]{1,0:T(8,128)(2,1)} %param.14) | copy-start | bytes 98308
Sparse Core Ops, SparseCore 0:
  9.8 84.0 all-gather.1
  366.4 33.2 reduce-scatter.1
where the time goes:
time: 412 us; the launch traced here: 408 us
  matrix products  100 us (24%)
  local copies, waits for them, and re-layouts  92.1 us (22%)
  waiting for transfers between devices  75.9 us (18%)
  other arithmetic  64.3 us (16%)
  blocking collectives  60.8 us (15%)
  between operations  13.6 us (3%)
    all_gather x1, waiting for transfers between devices, shards(): source_pairs = lax.all_gather(own_pairs, 'dst', axis=0, tiled=True)  67.3 us
    reduce_sum x16, other arithmetic, visit_slot(): new_sum = run_sum * factor + jnp.sum(weights, axis=2)  52.1 us
    dot_general x16, matrix products, visit_slot(): jnp.einsum('bhct,bchd->bthd', weights.astype(jnp.bfloat16), values_here,...  49.9 us
    dot_general x16, matrix products, visit_slot(): jnp.einsum('bchd,bthd->bhct', keys_here, query_blocks, preferred_element_...  47 us
    gather x16, local copies, waits for them, and re-layouts, visit_slot(): picked = jnp.take(pair_blocks, block_lists[:, slot_index], axis=0)  44.8 us
    pmax x1, blocking collectives, shards(): row_peak = lax.pmax(maxima, 'src')  23.6 us
    unnamed x1, blocking collectives  23.6 us
    shift_right_arithmetic x48, local copies, waits for them, and re-layouts, unpack_links(): jnp.right_shift(slot_words[:, :, None, :], bit_shifts[None, None, :, None])  16.2 us
  transfers between devices with their start and end apart: 2, of which 2 were waited for; matrix products, arithmetic and copies ran while one was open for 1% of the time, Pallas kernels for 0%

commit v1 on v0

v1 whole, which is shorter than its diff:
```python
import functools
import math

import jax
import jax.numpy as jnp
from jax import lax
from jax.experimental import pallas as pl
from jax.experimental.pallas import tpu as pltpu
from jax.sharding import PartitionSpec as P

HEADS = 4
BLK = 128
HEAD = 32
DESTS = 16
SLOTS = 16
ITEMS = 136
NEG = -1e30
MSG = 160
BF16 = jnp.bfloat16
F32 = jnp.float32
NT = (((1,), (1,)), ((), ()))
TN = (((0,), (0,)), ((), ()))


def vmem():
    return pl.BlockSpec(memory_space=pltpu.VMEM)


def smem():
    return pl.BlockSpec(memory_space=pltpu.SMEM)


def prep_kernel(rows_ref, wqt_ref, qbd_ref):
    scale = math.log2(math.e) / math.sqrt(HEAD)
    qbd_ref[...] = jnp.zeros_like(qbd_ref)

    def body(i, carry):
        rows = rows_ref[i]
        qt = lax.dot_general(wqt_ref[...], rows, NT, preferred_element_type=F32)
        qs = qt.astype(BF16).astype(F32) * scale
        high = qs.astype(BF16)
        low = (qs - high.astype(F32)).astype(BF16)
        for k in range(2):
            for h in range(HEADS):
                r = slice(h * HEAD, (h + 1) * HEAD)
                c = slice(h * BLK, (h + 1) * BLK)
                t = slice(k * BLK, (k + 1) * BLK)
                qbd_ref[2 * i + k, r, c] = high[r, t]
                qbd_ref[2 * i + k, BLK + h * HEAD : BLK + (h + 1) * HEAD, c] = low[r, t]
        return carry

    lax.fori_loop(0, DESTS // 2, body, 0)


def project(chunk_refs, wk_ref, wvt_ref, k_ref, vt_ref):
    for n, chunk_ref in enumerate(chunk_refs):
        per = chunk_ref.shape[0] // 256

        def body(i, carry, n=n, chunk_ref=chunk_ref, per=per):
            rows = chunk_ref[pl.ds(i * 256, 256), :]
            keys = jnp.dot(rows, wk_ref[...], preferred_element_type=F32).astype(BF16)
            vals = lax.dot_general(wvt_ref[...], rows, NT, preferred_element_type=F32).astype(BF16)
            at = (n * per + i) * 2
            for k in range(2):
                t = slice(k * BLK, (k + 1) * BLK)
                k_ref[at + k] = keys[t]
                vt_ref[at + k] = vals[:, t]
            return carry

        lax.fori_loop(0, per, body, 0)


def visit(items_ref, count, words_ref, qbd_ref, k_ref, vt_ref, m_ref, l_ref, acc_ref, s_ref, x_ref, w_ref, f_ref):
    sub_iota = lax.broadcasted_iota(jnp.int32, (8, BLK), 0)
    bit = jnp.left_shift(jnp.ones((8, BLK), jnp.int32), sub_iota)
    ones = jnp.ones((16, 2 * BLK), BF16)

    def fields(i):
        p1 = items_ref[0, i]
        p2 = items_ref[1, i]
        live1 = lax.shift_right_logical(p1, 16)
        live2 = lax.shift_right_logical(p2, 16)
        w1 = p1 & 255
        w2 = p2 & 255
        b1 = lax.shift_right_logical(p1, 8) & 255
        b2 = lax.shift_right_logical(p2, 8) & 255
        q = lax.shift_right_logical(w1, 4)
        return q, jnp.where(live1 == 1, q, DESTS), b1, b2, w1, w2, live1, live2

    def body(i, carry):
        _, qd, b1, b2, _, _, _, _ = fields(i)
        for p in range(2):
            r = slice(64 * p, 64 * p + 64)
            lhs = jnp.concatenate([vt_ref[b1, r, :], vt_ref[b2, r, :]], axis=1)
            lhs = jnp.concatenate([lhs, ones], axis=0)
            o = jnp.dot(lhs, w_ref[:, 256 * p : 256 * p + 256], preferred_element_type=F32)
            for k in range(2):
                h = 2 * p + k
                c = slice(BLK * k, BLK * k + BLK)
                fac = f_ref[h : h + 1, :]
                a = slice(h * HEAD, (h + 1) * HEAD)
                acc_ref[qd, a, :] = acc_ref[qd, a, :] * fac + o[k * HEAD : (k + 1) * HEAD, c]
                l_ref[qd, h : h + 1, :] = l_ref[qd, h : h + 1, :] * fac + o[64:65, c]
        _, qd, _, _, _, _, _, _ = fields(i + 1)
        for h in range(HEADS):
            c = slice(BLK * h, BLK * h + BLK)
            old = m_ref[qd, h : h + 1, :]
            new = jnp.maximum(old, x_ref[h : h + 1, :])
            f_ref[h : h + 1, :] = jnp.exp2(old - new)
            m_ref[qd, h : h + 1, :] = new
            w_ref[:, c] = jnp.exp2(s_ref[:, c] - new).astype(BF16)
        q, _, b1, b2, w1, w2, live1, live2 = fields(i + 2)
        kk = jnp.concatenate([k_ref[b1], k_ref[b2]], axis=0)
        lhs = jnp.concatenate([kk, kk], axis=1)
        words = [words_ref[w1] * live1, words_ref[w2] * live2]
        for p in range(2):
            s = jnp.dot(lhs, qbd_ref[q, :, 256 * p : 256 * p + 256], preferred_element_type=F32)
            peak = [None, None]
            for g in range(32):
                row = words[g // 16][g % 16 : g % 16 + 1, :]
                hit = (jnp.broadcast_to(row, (8, BLK)) & bit) != 0
                for k in range(2):
                    v = jnp.where(hit, s[8 * g : 8 * g + 8, BLK * k : BLK * k + BLK], NEG)
                    s_ref[8 * g : 8 * g + 8, 256 * p + BLK * k : 256 * p + BLK * k + BLK] = v
                    peak[k] = v if peak[k] is None else jnp.maximum(peak[k], v)
            for k in range(2):
                x_ref[2 * p + k : 2 * p + k + 1, :] = jnp.max(peak[k], axis=0, keepdims=True)
        return carry

    lax.fori_loop(0, count + 2, body, 0)


def phase_kernel(first, last, n_chunks, items_ref, count_ref, words_ref, qbd_ref, wk_ref, wvt_ref, *refs):
    chunks = refs[:n_chunks]
    refs = refs[n_chunks:]
    if first:
        state_in = None
    else:
        state_in, refs = refs[:3], refs[3:]
    if last:
        msg_ref, refs = refs[0], refs[1:]
    else:
        state_out, refs = refs[:3], refs[3:]
    k_ref, vt_ref, m_ref, l_ref, acc_ref, s_ref, x_ref, w_ref, f_ref = refs
    project(chunks, wk_ref, wvt_ref, k_ref, vt_ref)
    if first:
        m_ref[...] = jnp.full_like(m_ref, NEG)
        l_ref[...] = jnp.zeros_like(l_ref)
        acc_ref[...] = jnp.zeros_like(acc_ref)
    else:
        m_ref[:DESTS] = state_in[0][...]
        l_ref[:DESTS] = state_in[1][...]
        acc_ref[:DESTS] = state_in[2][...]
        m_ref[DESTS] = jnp.full((8, BLK), NEG, F32)
    s_ref[...] = jnp.zeros_like(s_ref)
    w_ref[...] = jnp.zeros_like(w_ref)
    x_ref[...] = jnp.zeros_like(x_ref)
    f_ref[...] = jnp.zeros_like(f_ref)
    visit(items_ref, count_ref[0], words_ref, qbd_ref, k_ref, vt_ref, m_ref, l_ref, acc_ref, s_ref, x_ref, w_ref, f_ref)
    if last:
        def emit(q, carry):
            top = m_ref[q, :HEADS, :]
            tot = l_ref[q, :HEADS, :]
            for h in range(HEADS):
                a = slice(h * HEAD, (h + 1) * HEAD)
                msg_ref[q, a, :] = (acc_ref[q, a, :] / tot[h : h + 1, :]).astype(BF16)
            parts = []
            for v in (top, tot):
                for _ in range(3):
                    piece = v.astype(BF16).astype(F32)
                    parts.append(piece)
                    v = v - piece
            parts.append(jnp.zeros((8, BLK), F32))
            msg_ref[q, BLK:, :] = jnp.concatenate(parts, axis=0).astype(BF16)
            return carry

        lax.fori_loop(0, DESTS, emit, 0)
    else:
        state_out[0][...] = m_ref[:DESTS]
        state_out[1][...] = l_ref[:DESTS]
        state_out[2][...] = acc_ref[:DESTS]


def run_phase(first, last, items, count, words, qbd, wk, wvt, chunks, state):
    blocks = sum(c.shape[0] for c in chunks) // BLK
    state_shape = (
        jax.ShapeDtypeStruct((DESTS, 8, BLK), F32),
        jax.ShapeDtypeStruct((DESTS, 8, BLK), F32),
        jax.ShapeDtypeStruct((DESTS, BLK, BLK), F32),
    )
    out_shape = jax.ShapeDtypeStruct((DESTS, MSG, BLK), BF16) if last else state_shape
    n_in = 6 + len(chunks) + (0 if first else 3)
    return pl.pallas_call(
        functools.partial(phase_kernel, first, last, len(chunks)),
        out_shape=out_shape,
        in_specs=[smem(), smem()] + [vmem()] * (n_in - 2),
        out_specs=vmem() if last else (vmem(),) * 3,
        scratch_shapes=[
            pltpu.VMEM((blocks, BLK, BLK), BF16),
            pltpu.VMEM((blocks, BLK, BLK), BF16),
            pltpu.VMEM((DESTS + 1, 8, BLK), F32),
            pltpu.VMEM((DESTS + 1, 8, BLK), F32),
            pltpu.VMEM((DESTS + 1, BLK, BLK), F32),
            pltpu.VMEM((2 * BLK, HEADS * BLK), F32),
            pltpu.VMEM((8, BLK), F32),
            pltpu.VMEM((2 * BLK, HEADS * BLK), BF16),
            pltpu.VMEM((8, BLK), F32),
        ],
        compiler_params=pltpu.CompilerParams(vmem_limit_bytes=40 * 1024 * 1024),
        cost_estimate=pl.CostEstimate(flops=500_000_000, bytes_accessed=8_000_000, transcendentals=4_000_000),
    )(items, count, words, qbd, wk, wvt, *chunks, *(() if first else state))


def combine_kernel(msg_ref, wo_ref, out_ref):
    sources = msg_ref.shape[0]
    for b in range(2):
        stats = []
        for j in range(sources):
            st = msg_ref[j, b, BLK:, :].astype(F32)
            stats.append((st[0:4] + st[4:8] + st[8:12], st[12:16] + st[16:20] + st[20:24]))
        peak = functools.reduce(jnp.maximum, [s[0] for s in stats])
        mass = [tot * jnp.exp2(top - peak) for top, tot in stats]
        denom = functools.reduce(jnp.add, mass)
        rows = []
        for h in range(HEADS):
            a = slice(h * HEAD, (h + 1) * HEAD)
            num = functools.reduce(
                jnp.add,
                [msg_ref[j, b, a, :].astype(F32) * mass[j][h : h + 1, :] for j in range(sources)],
            )
            rows.append(num / denom[h : h + 1, :])
        att = jnp.concatenate(rows, axis=0).astype(BF16)
        mixed = lax.dot_general(att, wo_ref[...], TN, preferred_element_type=F32)
        out_ref[b * BLK : (b + 1) * BLK, :] = mixed.astype(BF16)


def make_items(lists, counts, my_dst):
    my_x, my_z = my_dst // 8, my_dst % 8
    owner = lists // 2
    dx = (owner // 8 - my_x) % 4
    dz = (owner % 8 - my_z) % 8
    at_z = 2 * jnp.minimum(dz, 8 - dz) - (dz >= 4).astype(jnp.int32)
    chunk = jnp.where(dx == 1, 1, 0)
    pos = (chunk * 8 + at_z) * 2 + lists % 2
    phase = jnp.where(dx == 0, 0, jnp.where(dx == 2, 2, 1))
    slots = jnp.arange(SLOTS, dtype=jnp.int32)
    dests = jnp.arange(DESTS, dtype=jnp.int32)
    word = dests[:, None] * SLOTS + slots[None, :]
    live = slots[None, :] < counts[:, None]
    pay = word | (pos << 8) | (1 << 16)
    sel = live[None] & (phase[None] == jnp.arange(3, dtype=jnp.int32)[:, None, None])
    sel_i = sel.astype(jnp.int32)
    before = (slots[None, :] < slots[:, None]).astype(jnp.int32)
    rank = jnp.sum(sel_i[:, :, None, :] * before[None, None], axis=-1)
    per_dest = (jnp.sum(sel_i, axis=-1) + 1) // 2
    offset = jnp.sum(per_dest[:, None, :] * before[None], axis=-1)
    total = jnp.sum(per_dest, axis=-1)
    item = jnp.where(sel, offset[:, :, None] + rank // 2 + 2, -1)
    key = (item * 2 + rank % 2).reshape(3, 1, DESTS * SLOTS)
    want = jnp.arange(2 * ITEMS, dtype=jnp.int32)
    want = (want % ITEMS) * 2 + want // ITEMS
    table = jnp.sum(jnp.where(key == want[None, :, None], pay.reshape(1, 1, -1), 0), axis=-1)
    return table.reshape(3, 2, ITEMS), total


def z_step(rows, step):
    return lax.ppermute(rows, "dst", [(x * 8 + z, x * 8 + (z + step) % 8) for x in range(4) for z in range(8)])


def x_step(rows, step):
    return lax.ppermute(rows, "dst", [(x * 8 + z, ((x + step) % 4) * 8 + z) for x in range(4) for z in range(8)])


def shards(node_feats, w_query, w_key, w_value, w_out, src_blocks, live_counts, edge_bits):
    own = node_feats[0, 0]
    near = [own] + [z_step(own, s) for s in (1, -1, 2, -2, 3, -3, 4)]
    base = jnp.concatenate(near, axis=0)
    left = x_step(base, 1)
    right = x_step(base, -1)
    far = x_step(base, 2)
    dest_rows = lax.all_gather(own, "src", axis=0, tiled=False)
    items, total = make_items(src_blocks[0, 0], live_counts[0, 0], lax.axis_index("dst"))
    words = edge_bits[0, 0].reshape(DESTS * SLOTS, 16, BLK)
    qbd = pl.pallas_call(
        prep_kernel,
        out_shape=jax.ShapeDtypeStruct((DESTS, 2 * BLK, HEADS * BLK), BF16),
        in_specs=[vmem(), vmem()],
        out_specs=vmem(),
    )(dest_rows, w_query.T)
    wvt = w_value.T
    run = functools.partial(run_phase, words=words, qbd=qbd, wk=w_key, wvt=wvt)
    state = run(True, False, items[0], total[0:1], chunks=[base], state=None)
    state = run(False, False, items[1], total[1:2], chunks=[left, right], state=state)
    msg = run(False, True, items[2], total[2:3], chunks=[far], state=state)
    got = lax.all_to_all(msg.reshape(8, 2, MSG, BLK), "src", 0, 0, tiled=True)
    mixed = pl.pallas_call(
        combine_kernel,
        out_shape=jax.ShapeDtypeStruct((2 * BLK, BLK), BF16),
        in_specs=[vmem(), vmem()],
        out_specs=vmem(),
    )(got, w_out)
    return mixed.reshape(1, 1, 2 * BLK, BLK)


def solution(mesh):
    in_specs = (
        P("src", "dst", None, None),
        P(),
        P(),
        P(),
        P(),
        P("src", "dst", None, None),
        P("src", "dst", None),
        P("src", "dst", None, None, None, None),
    )
    out_specs = P("src", "dst", None, None)
    return jax.shard_map(shards, mesh=mesh, in_specs=in_specs, out_specs=out_specs, check_vma=False)
```

time: 412 us -> 127 us (0.31)
  matrix products: 100 us -> 0 us
  local copies, waits for them, and re-layouts: 92.1 us -> 13.4 us
  waiting for transfers between devices: 75.9 us -> 9.82 us
  other arithmetic: 64.3 us -> 3.23 us
  Pallas kernels: 0 us -> 27 us
  starting transfers between devices: 0.04 us -> 18.4 us
  between operations: 13.6 us -> 0.13 us
  blocking collectives: 60.8 us -> 53 us
    dot_general x35 -> x0, matrix products: 100 us -> none  [the longest x16 49.9 us: visit_slot(): jnp.einsum('bhct,bchd->bthd', weights.astype(jnp.bfloat16), values_here,...]
    all_gather x1 -> x0, waiting for transfers between devices: 67.3 us -> none  [shards(): source_pairs = lax.all_gather(own_pairs, 'dst', axis=0, tiled=True)]
    reduce_sum x16 -> x5, other arithmetic: 52.1 us -> 1.66 us  [the longest x1 0.89 us: make_items(): rank = jnp.sum(sel_i[:, :, None, :] * before[None, None], axis=-1)]
    gather x16 -> x0, local copies, waits for them, and re-layouts: 44.8 us -> none  [visit_slot(): picked = jnp.take(pair_blocks, block_lists[:, slot_index], axis=0)]
    all_to_all x0 -> x1, blocking collectives: none -> 38.1 us  [shards(): got = lax.all_to_all(msg.reshape(8, 2, MSG, BLK), 'src', 0, 0, tiled=True)]
    pallas_call x0 -> x5, Pallas kernels: none -> 27 us  [the longest x3 20.3 us: run_phase(): pl.pallas_call(functools.partial(phase_kernel, first, last, len(chunks)),...]
    pmax x1 -> x0, blocking collectives: 23.6 us -> none  [shards(): row_peak = lax.pmax(maxima, 'src')]
    unnamed x1 -> x0, blocking collectives: 23.6 us -> none
  transfers between devices with their start and end apart: 2 -> 10, of which waited for: 2 -> 2; matrix products, arithmetic and copies ran while one was open for 1% -> 11% of each run, Pallas kernels for 0% -> 15%
where the time goes in v1:
time: 127 us; the launch traced here: 125 us
  blocking collectives  53 us (42%)
  Pallas kernels  27 us (21%)
  starting transfers between devices  18.4 us (14%)
  local copies, waits for them, and re-layouts  13.4 us (11%)
  waiting for transfers between devices  9.82 us (8%)
  other arithmetic  3.23 us (3%)
    all_to_all x1, blocking collectives, shards(): got = lax.all_to_all(msg.reshape(8, 2, MSG, BLK), 'src', 0, 0, tiled=True)  38.1 us
    pallas_call x3, Pallas kernels, run_phase(): pl.pallas_call(functools.partial(phase_kernel, first, last, len(chunks)),...  20.3 us
    all_gather x1, blocking collectives, shards(): dest_rows = lax.all_gather(own, 'src', axis=0, tiled=False)  14.9 us
    ppermute x7, starting transfers between devices, z_step(): lax.ppermute(rows, 'dst', [(x * 8 + z, x * 8 + (z + step) % 8) for x in r...  13.3 us
    ppermute x7, waiting for transfers between devices, z_step(): lax.ppermute(rows, 'dst', [(x * 8 + z, x * 8 + (z + step) % 8) for x in r...  9.82 us
    unnamed x15, local copies, waits for them, and re-layouts  9.74 us
    ppermute x3, starting transfers between devices, x_step(): lax.ppermute(rows, 'dst', [(x * 8 + z, (x + step) % 4 * 8 + z) for x in r...  5.13 us
    pallas_call x1, Pallas kernels, shards(): pl.pallas_call(prep_kernel, out_shape=jax.ShapeDtypeStruct((DESTS, 2 * BL...  4.72 us
  transfers between devices with their start and end apart: 10, of which 2 were waited for; matrix products, arithmetic and copies ran while one was open for 11% of the time, Pallas kernels for 15%

profile of v1, /device:TPU:96, one launch (start us, length us, event | category | flops | bytes accessed | tf_op | source)
XLA Modules:
  0.0 125.1 jit_solution(10926013756822545612)
XLA Ops:
  0.0 4.5 %collective-permute-start.6 = (bf16[256,128]{1,0:T(8,128)(2,1)}, bf16[256,128]{1,0:T(8,128)(2,1)S(1)}, u32[]{:S(2)}, u32[]{:S(2)}) collective-permute-start(bf16[256,128]{1,0:T(8,128)(2,1)} %bitcast.39), channel_id=1, source_target_pairs={{0,32},{8,40},{16,48},{24,56},{32,0},{40,8},{48,16},{56,24},{64,96... | collective-permute-start | bytes 196616 | tf_op jit(solution)/shard_map/ppermute | solution.py:267
  4.5 1.9 %collective-permute-start.5 = (bf16[256,128]{1,0:T(8,128)(2,1)}, bf16[256,128]{1,0:T(8,128)(2,1)S(1)}, u32[]{:S(2)}, u32[]{:S(2)}) collective-permute-start(bf16[256,128]{1,0:T(8,128)(2,1)} %bitcast.40), channel_id=1, source_target_pairs={{0,40},{8,48},{16,56},{24,0},{32,8},{40,16},{48,24},{56,32},{64,10... | collective-permute-start | bytes 196616 | tf_op jit(solution)/shard_map/ppermute | solution.py:267
  6.4 3.1 %collective-permute-start.4 = (bf16[256,128]{1,0:T(8,128)(2,1)}, bf16[256,128]{1,0:T(8,128)(2,1)S(1)}, u32[]{:S(2)}, u32[]{:S(2)}) collective-permute-start(bf16[256,128]{1,0:T(8,128)(2,1)} %bitcast.41), channel_id=1, source_target_pairs={{0,24},{8,32},{16,40},{24,48},{32,56},{40,0},{48,8},{56,16},{64,88... | collective-permute-start | bytes 196616 | tf_op jit(solution)/shard_map/ppermute | solution.py:267
  9.5 1.5 %collective-permute-start.3 = (bf16[256,128]{1,0:T(8,128)(2,1)}, bf16[256,128]{1,0:T(8,128)(2,1)S(1)}, u32[]{:S(2)}, u32[]{:S(2)}) collective-permute-start(bf16[256,128]{1,0:T(8,128)(2,1)} %bitcast.42), channel_id=1, source_target_pairs={{0,48},{8,56},{16,0},{24,8},{32,16},{40,24},{48,32},{56,40},{64,11... | collective-permute-start | bytes 196616 | tf_op jit(solution)/shard_map/ppermute | solution.py:267
  11.0 2.2 %collective-permute-start = (bf16[256,128]{1,0:T(8,128)(2,1)}, bf16[256,128]{1,0:T(8,128)(2,1)S(1)}, u32[]{:S(2)}, u32[]{:S(2)}) collective-permute-start(bf16[256,128]{1,0:T(8,128)(2,1)} %bitcast.43), channel_id=1, source_target_pairs={{0,8},{8,16},{16,24},{24,32},{32,40},{40,48},{48,56},{56,0},{64,72... | collective-permute-start | bytes 196616 | tf_op jit(solution)/shard_map/ppermute | solution.py:267
  13.2 0.7 iota_compare_fusion.2
  14.0 0.7 broadcast_reduce_fusion
  14.7 0.8 squeeze.17
  16.4 1.5 %constant_dynamic-update-slice_fusion.7 = bf16[2048,128]{1,0:T(8,128)(2,1)} fusion(bf16[1,1,256,128]{3,2,1,0:T(8,128)(2,1)} %param.8), kind=kLoop, calls=%fused_computation.13 | loop fusion | bytes 131072
  18.5 0.9 multiply_reduce_fusion
  20.4 5.1 %collective-permute-done.1 = bf16[256,128]{1,0:T(8,128)(2,1)S(1)} collective-permute-done((bf16[256,128]{1,0:T(8,128)(2,1)}, bf16[256,128]{1,0:T(8,128)(2,1)S(1)}, u32[]{:S(2)}, u32[]{:S(2)}) %collective-permute-start.1) | collective-permute-done | bytes 65568 | tf_op jit(solution)/shard_map/ppermute | solution.py:267
  26.1 4.8 %collective-permute-done.2 = bf16[256,128]{1,0:T(8,128)(2,1)S(1)} collective-permute-done((bf16[256,128]{1,0:T(8,128)(2,1)}, bf16[256,128]{1,0:T(8,128)(2,1)S(1)}, u32[]{:S(2)}, u32[]{:S(2)}) %collective-permute-start.2) | collective-permute-done | bytes 65568 | tf_op jit(solution)/shard_map/ppermute | solution.py:267
  34.0 2.8 %collective-permute-start.9 = (bf16[2048,128]{1,0:T(8,128)(2,1)}, bf16[2048,128]{1,0:T(8,128)(2,1)S(1)}, u32[]{:S(2)}, u32[]{:S(2)}) collective-permute-start(bf16[2048,128]{1,0:T(8,128)(2,1)} %constant_dynamic-update-slice_fusion.refs_0_), channel_id=1, source_target_pairs={{0,192},{8,200},{16,208},{24,216},{32,224},{40,232},{48,240},{56,2... | collective-permute-start | bytes 1572872 | tf_op jit(solution)/shard_map/ppermute | solution.py:271
  37.1 2.4 %collective-permute-start.7 = (bf16[2048,128]{1,0:T(8,128)(2,1)}, bf16[2048,128]{1,0:T(8,128)(2,1)S(1)}, u32[]{:S(2)}, u32[]{:S(2)}) collective-permute-start(bf16[2048,128]{1,0:T(8,128)(2,1)} %constant_dynamic-update-slice_fusion.refs_0_), channel_id=1, source_target_pairs={{0,128},{8,136},{16,144},{24,152},{32,160},{40,168},{48,176},{56,1... | collective-permute-start | bytes 1572872 | tf_op jit(solution)/shard_map/ppermute | solution.py:271
  39.7 1.5 %copy.14 = bf16[128,128]{0,1:T(8,128)(2,1)} copy(bf16[128,128]{1,0:T(8,128)(2,1)} %param.9) | data formatting | bytes 65536 | tf_op args[1]
  41.2 0.9 copy.15
  42.1 14.9 %all-gather = bf16[8,1,256,128]{3,2,1,0:T(8,128)(2,1)} all-gather(bf16[1,1,256,128]{3,2,1,0:T(8,128)(2,1)} %param.8), channel_id=2, replica_groups=mesh['dst'=32,'src'=8] {'src'}, dimensions={0}, use_global_device_ids=true | all-gather | bytes 589824 | tf_op jit(solution)/shard_map/all_gather | solution.py:281
  57.0 4.7 %shard_map.82.qbd_ref = bf16[16,256,512]{2,1,0:T(8,128)(2,1)} custom-call(bf16[8,256,128]{2,1,0:T(8,128)(2,1)} %bitcast.38, bf16[128,128]{1,0:T(8,128)(2,1)} %bitcast.46), custom_call_target="tpu_custom_call" | custom-call | tf_op jit(solution)/shard_map/pallas_call | solution.py:284
  62.4 2.2 %copy-done = bf16[16,256,512]{2,1,0:T(8,128)(2,1)S(1)} copy-done((bf16[16,256,512]{2,1,0:T(8,128)(2,1)S(1)}, bf16[16,256,512]{2,1,0:T(8,128)(2,1)}, u32[]{:S(2)}) %copy-start) | copy-done | bytes 4194328
  64.6 6.1 %shard_map.83 = (f32[16,8,128]{2,1,0:T(8,128)S(1)}, f32[16,8,128]{2,1,0:T(8,128)S(1)}, f32[16,128,128]{2,1,0:T(8,128)S(1)}) custom-call(s32[2,136]{1,0:T(2,128)S(1)} %squeeze.22.items_ref, s32[1]{0:T(128)} %get-tuple-element.24.count_ref, s32[256,16,128]{2,1,0:T(8,128)S(1)} %bitcast.31, bf16[16,256,512]{2,1,0:T(8,128)(2,1)S(1)} %copy-done, ...), custom_call_target="tpu_custom_call" | custom-call | flops 500000000 | bytes 8000000 | tf_op jit(solution)/shard_map/pallas_call | solution.py:193
  70.6 8.3 %shard_map.84 = (f32[16,8,128]{2,1,0:T(8,128)S(1)}, f32[16,8,128]{2,1,0:T(8,128)S(1)}, f32[16,128,128]{2,1,0:T(8,128)S(1)}) custom-call(s32[2,136]{1,0:T(2,128)S(1)} %squeeze.21.items_ref, s32[1]{0:T(128)} %get-tuple-element.25.count_ref, s32[256,16,128]{2,1,0:T(8,128)S(1)} %bitcast.32, bf16[16,256,512]{2,1,0:T(8,128)(2,1)S(1)} %copy-done, ...), custom_call_target="tpu_custom_call" | custom-call | flops 500000000 | bytes 8000000 | tf_op jit(solution)/shard_map/pallas_call | solution.py:193
  79.0 5.9 %shard_map.85 = bf16[16,160,128]{2,1,0:T(8,128)(2,1)S(1)} custom-call(s32[2,136]{1,0:T(2,128)S(1)} %squeeze.19.items_ref, s32[1]{0:T(128)} %get-tuple-element.26.count_ref, s32[256,16,128]{2,1,0:T(8,128)S(1)} %bitcast.33, bf16[16,256,512]{2,1,0:T(8,128)(2,1)S(1)} %copy-done, bf16[128,128]{1,0:T(8,128)(2,1)S(1)} %copy-done.2, bf16[128,128]{1,0:T(8,128)(2,1)S(1)} %bitcast.37, ...), custom_call_target="tpu_custom_call" | custom-call | flops 500000000 | bytes 8000000 | tf_op jit(solution)/shard_map/pallas_call | solution.py:193
  84.9 38.1 %all_to_all.5.msg_ref = bf16[8,2,160,128]{3,2,1,0:T(8,128)(2,1)} all-to-all(bf16[8,2,160,128]{3,2,1,0:T(8,128)(2,1)S(1)} %bitcast.34), channel_id=1, replica_groups=mesh['dst'=32,'src'=8] {'src'}, dimensions={0} | all-to-all | bytes 1310720 | tf_op jit(solution)/shard_map/all_to_all | solution.py:295
  123.0 2.1 %shard_map.86 = bf16[256,128]{1,0:T(8,128)(2,1)} custom-call(bf16[8,2,160,128]{3,2,1,0:T(8,128)(2,1)} %all_to_all.5.msg_ref, bf16[128,128]{1,0:T(8,128)(2,1)} %wo_ref.1), custom_call_target="tpu_custom_call" | custom-call | tf_op jit(solution)/shard_map/pallas_call | solution.py:296
  (49 shorter events, 7.6 us)
Async XLA Ops:
  0.0 62.4 %copy-start.2 = (bf16[128,128]{1,0:T(8,128)(2,1)S(1)}, bf16[128,128]{1,0:T(8,128)(2,1)}, u32[]{:S(2)}) copy-start(bf16[128,128]{1,0:T(8,128)(2,1)} %wk_ref.5) | copy-start | bytes 98308
  0.0 62.4 %copy-start.1 = (s32[1,1,16,16,16,128]{5,4,3,2,1,0:T(8,128)S(1)}, s32[1,1,16,16,16,128]{5,4,3,2,1,0:T(8,128)}, u32[]{:S(2)}) copy-start(s32[1,1,16,16,16,128]{5,4,3,2,1,0:T(8,128)} %param.15) | copy-start | bytes 6291460
  0.0 33.3 %collective-permute-start.6 = (bf16[256,128]{1,0:T(8,128)(2,1)}, bf16[256,128]{1,0:T(8,128)(2,1)S(1)}, u32[]{:S(2)}, u32[]{:S(2)}) collective-permute-start(bf16[256,128]{1,0:T(8,128)(2,1)} %bitcast.39), channel_id=1, source_target_pairs={{0,32},{8,40},{16,48},{24,56},{32,0},{40,8},{48,16},{56,24},{64,96... | collective-permute-start | bytes 196616 | tf_op jit(solution)/shard_map/ppermute | solution.py:267
  4.5 28.2 %collective-permute-start.5 = (bf16[256,128]{1,0:T(8,128)(2,1)}, bf16[256,128]{1,0:T(8,128)(2,1)S(1)}, u32[]{:S(2)}, u32[]{:S(2)}) collective-permute-start(bf16[256,128]{1,0:T(8,128)(2,1)} %bitcast.40), channel_id=1, source_target_pairs={{0,40},{8,48},{16,56},{24,0},{32,8},{40,16},{48,24},{56,32},{64,10... | collective-permute-start | bytes 196616 | tf_op jit(solution)/shard_map/ppermute | solution.py:267
  6.4 25.7 %collective-permute-start.4 = (bf16[256,128]{1,0:T(8,128)(2,1)}, bf16[256,128]{1,0:T(8,128)(2,1)S(1)}, u32[]{:S(2)}, u32[]{:S(2)}) collective-permute-start(bf16[256,128]{1,0:T(8,128)(2,1)} %bitcast.41), channel_id=1, source_target_pairs={{0,24},{8,32},{16,40},{24,48},{32,56},{40,0},{48,8},{56,16},{64,88... | collective-permute-start | bytes 196616 | tf_op jit(solution)/shard_map/ppermute | solution.py:267
  9.5 21.9 %collective-permute-start.3 = (bf16[256,128]{1,0:T(8,128)(2,1)}, bf16[256,128]{1,0:T(8,128)(2,1)S(1)}, u32[]{:S(2)}, u32[]{:S(2)}) collective-permute-start(bf16[256,128]{1,0:T(8,128)(2,1)} %bitcast.42), channel_id=1, source_target_pairs={{0,48},{8,56},{16,0},{24,8},{32,16},{40,24},{48,32},{56,40},{64,11... | collective-permute-start | bytes 196616 | tf_op jit(solution)/shard_map/ppermute | solution.py:267
  11.0 8.7 %collective-permute-start = (bf16[256,128]{1,0:T(8,128)(2,1)}, bf16[256,128]{1,0:T(8,128)(2,1)S(1)}, u32[]{:S(2)}, u32[]{:S(2)}) collective-permute-start(bf16[256,128]{1,0:T(8,128)(2,1)} %bitcast.43), channel_id=1, source_target_pairs={{0,8},{8,16},{16,24},{24,32},{32,40},{40,48},{48,56},{56,0},{64,72... | collective-permute-start | bytes 196616 | tf_op jit(solution)/shard_map/ppermute | solution.py:267
  19.7 5.8 %collective-permute-start.1 = (bf16[256,128]{1,0:T(8,128)(2,1)}, bf16[256,128]{1,0:T(8,128)(2,1)S(1)}, u32[]{:S(2)}, u32[]{:S(2)}) collective-permute-start(bf16[256,128]{1,0:T(8,128)(2,1)} %bitcast.44), channel_id=1, source_target_pairs={{0,56},{8,0},{16,8},{24,16},{32,24},{40,32},{48,40},{56,48},{64,12... | collective-permute-start | bytes 196616 | tf_op jit(solution)/shard_map/ppermute | solution.py:267
  25.5 5.4 %collective-permute-start.2 = (bf16[256,128]{1,0:T(8,128)(2,1)}, bf16[256,128]{1,0:T(8,128)(2,1)S(1)}, u32[]{:S(2)}, u32[]{:S(2)}) collective-permute-start(bf16[256,128]{1,0:T(8,128)(2,1)} %bitcast.45), channel_id=1, source_target_pairs={{0,16},{8,24},{16,32},{24,40},{32,48},{40,56},{48,0},{56,8},{64,80... | collective-permute-start | bytes 196616 | tf_op jit(solution)/shard_map/ppermute | solution.py:267
  34.0 36.7 %collective-permute-start.9 = (bf16[2048,128]{1,0:T(8,128)(2,1)}, bf16[2048,128]{1,0:T(8,128)(2,1)S(1)}, u32[]{:S(2)}, u32[]{:S(2)}) collective-permute-start(bf16[2048,128]{1,0:T(8,128)(2,1)} %constant_dynamic-update-slice_fusion.refs_0_), channel_id=1, source_target_pairs={{0,192},{8,200},{16,208},{24,216},{32,224},{40,232},{48,240},{56,2... | collective-permute-start | bytes 1572872 | tf_op jit(solution)/shard_map/ppermute | solution.py:271
  36.7 33.9 %collective-permute-start.8 = (bf16[2048,128]{1,0:T(8,128)(2,1)}, bf16[2048,128]{1,0:T(8,128)(2,1)}, u32[]{:S(2)}, u32[]{:S(2)}) collective-permute-start(bf16[2048,128]{1,0:T(8,128)(2,1)} %constant_dynamic-update-slice_fusion.refs_0_), channel_id=1, source_target_pairs={{0,64},{8,72},{16,80},{24,88},{32,96},{40,104},{48,112},{56,120},{... | collective-permute-start | bytes 1572872 | tf_op jit(solution)/shard_map/ppermute | solution.py:271
  37.1 41.9 %collective-permute-start.7 = (bf16[2048,128]{1,0:T(8,128)(2,1)}, bf16[2048,128]{1,0:T(8,128)(2,1)S(1)}, u32[]{:S(2)}, u32[]{:S(2)}) collective-permute-start(bf16[2048,128]{1,0:T(8,128)(2,1)} %constant_dynamic-update-slice_fusion.refs_0_), channel_id=1, source_target_pairs={{0,128},{8,136},{16,144},{24,152},{32,160},{40,168},{48,176},{56,1... | collective-permute-start | bytes 1572872 | tf_op jit(solution)/shard_map/ppermute | solution.py:271
  62.4 2.2 %copy-start = (bf16[16,256,512]{2,1,0:T(8,128)(2,1)S(1)}, bf16[16,256,512]{2,1,0:T(8,128)(2,1)}, u32[]{:S(2)}) copy-start(bf16[16,256,512]{2,1,0:T(8,128)(2,1)} %shard_map.82.qbd_ref) | copy-start | bytes 12582916

commit v2 on v1

v2 whole, which is shorter than its diff:
```python
import functools
import math

import jax
import jax.numpy as jnp
from jax import lax
from jax.experimental import pallas as pl
from jax.experimental.pallas import tpu as pltpu
from jax.sharding import PartitionSpec as P

HEADS = 4
BLK = 128
HEAD = 32
DESTS = 16
SLOTS = 16
ITEMS = 144
NEG = -1e30
MSG = 144
LIMIT = 100.0
SCALE = math.log2(math.e) / math.sqrt(HEAD)
BF16 = jnp.bfloat16
F32 = jnp.float32
NT = (((1,), (1,)), ((), ()))
TN = (((0,), (0,)), ((), ()))


def vmem():
    return pl.BlockSpec(memory_space=pltpu.VMEM)


def smem():
    return pl.BlockSpec(memory_space=pltpu.SMEM)


def copy_kernel(own_ref, out_ref):
    for i in range(8):
        out_ref[i] = own_ref[...]


def prep_kernel(me_ref, *refs):
    row_refs, (wq_ref, wv_ref, qbd_ref, wvt_ref, qnorm_ref) = refs[:8], refs[8:]
    qbd_ref[...] = jnp.zeros_like(qbd_ref)
    wvt_ref[...] = wv_ref[...].T
    wqt = wq_ref[...].T
    norm = jnp.zeros((HEADS, 2 * BLK), F32)
    for step in range(8):
        owner = (me_ref[0] - step) & 7
        qt = lax.dot_general(wqt, row_refs[step][...], NT, preferred_element_type=F32).astype(BF16)
        wide = qt.astype(F32)
        norm = jnp.maximum(norm, jnp.sum((wide * wide).reshape(HEADS, HEAD, 2 * BLK), axis=1))
        for k in range(2):
            for h in range(HEADS):
                r = slice(h * HEAD, (h + 1) * HEAD)
                qbd_ref[2 * owner + k, r, h * BLK : (h + 1) * BLK] = qt[r, k * BLK : (k + 1) * BLK]
    qnorm_ref[...] = norm


def project(chunk_refs, wk_ref, wvt_ref, k_ref, vt_ref, norm_ref):
    col = lax.shift_right_logical(lax.broadcasted_iota(jnp.int32, (BLK, BLK), 0), 5)
    row = lax.shift_right_logical(lax.broadcasted_iota(jnp.int32, (BLK, BLK), 1), 5)
    same = (col == row).astype(BF16)
    norm_ref[...] = jnp.zeros_like(norm_ref)
    for n, chunk_ref in enumerate(chunk_refs):
        per = chunk_ref.shape[0] // 512

        def body(i, carry, n=n, chunk_ref=chunk_ref, per=per):
            rows = chunk_ref[pl.ds(i * 512, 512), :]
            keys = jnp.dot(rows, wk_ref[...], preferred_element_type=F32).astype(BF16)
            vals = lax.dot_general(wvt_ref[...], rows, NT, preferred_element_type=F32).astype(BF16)
            wide = keys.astype(F32)
            norms = jnp.dot((wide * wide).astype(BF16), same, preferred_element_type=F32)
            norm_ref[...] = jnp.maximum(norm_ref[...], jnp.max(norms.reshape(64, 8, BLK), axis=0))
            at = (n * per + i) * 4
            for k in range(4):
                t = slice(k * BLK, (k + 1) * BLK)
                k_ref[at + k] = keys[t]
                vt_ref[at + k] = vals[:, t]
            return carry

        lax.fori_loop(0, per, body, 0, unroll=4)


def fields(items_ref, i):
    p1 = items_ref[0, i]
    p2 = items_ref[1, i]
    live1 = lax.shift_right_logical(p1, 16)
    live2 = lax.shift_right_logical(p2, 16)
    w1 = p1 & 255
    w2 = p2 & 255
    b1 = lax.shift_right_logical(p1, 8) & 255
    b2 = lax.shift_right_logical(p2, 8) & 255
    q = lax.shift_right_logical(w1, 4)
    return q, jnp.where(live1 == 1, q, DESTS), b1, b2, w1, w2, live1, live2


def bit_of_row():
    sub_iota = lax.broadcasted_iota(jnp.int32, (8, BLK), 0)
    return jnp.left_shift(jnp.ones((8, BLK), jnp.int32), sub_iota)


def visit_bounded(items_ref, count, words_ref, qbd_ref, k_ref, vt_ref, l_ref, acc_ref, w_refs):
    bit = bit_of_row()
    ones = jnp.ones((16, 2 * BLK), BF16)

    def gather_values(i, w_ref):
        _, qd, b1, b2, _, _, _, _ = fields(items_ref, i)
        for p in range(2):
            r = slice(64 * p, 64 * p + 64)
            lhs = jnp.concatenate([vt_ref[b1, r, :], vt_ref[b2, r, :]], axis=1)
            lhs = jnp.concatenate([lhs, ones], axis=0)
            o = jnp.dot(lhs, w_ref[:, 256 * p : 256 * p + 256], preferred_element_type=F32)
            for k in range(2):
                h = 2 * p + k
                c = slice(BLK * k, BLK * k + BLK)
                a = slice(h * HEAD, (h + 1) * HEAD)
                acc_ref[qd, a, :] += o[k * HEAD : (k + 1) * HEAD, c]
                l_ref[qd, h : h + 1, :] += o[64:65, c]

    def weigh(i, w_ref):
        q, _, b1, b2, w1, w2, live1, live2 = fields(items_ref, i)
        kk = jnp.concatenate([k_ref[b1], k_ref[b2]], axis=0)
        words = [words_ref[w1] * live1, words_ref[w2] * live2]
        for p in range(2):
            s = jnp.dot(kk, qbd_ref[q, :, 256 * p : 256 * p + 256], preferred_element_type=F32)
            for g in range(16):
                hits = []
                for u in (2 * g, 2 * g + 1):
                    line = words[u // 16][u % 16 : u % 16 + 1, :]
                    hits.append((jnp.broadcast_to(line, (8, BLK)) & bit) != 0)
                for k in range(2):
                    v = [
                        jnp.exp2(jnp.where(hits[u], s[16 * g + 8 * u : 16 * g + 8 * u + 8, BLK * k : BLK * k + BLK] * SCALE, NEG))
                        for u in range(2)
                    ]
                    c = slice(256 * p + BLK * k, 256 * p + BLK * k + BLK)
                    w_ref[16 * g : 16 * g + 16, c] = jnp.concatenate(v, axis=0).astype(BF16)

    def body(j, carry):
        for e in range(4):
            i = 4 * j + e
            weigh(i + 2, w_refs[e % 2])
            gather_values(i + 1, w_refs[1 - e % 2])
        return carry

    lax.fori_loop(0, lax.shift_right_logical(count + 4, 2), body, 0)


def visit(items_ref, count, words_ref, qbd_ref, k_ref, vt_ref, m_ref, l_ref, acc_ref, s_refs, x_refs, w_refs, f_refs):
    bit = bit_of_row()
    ones = jnp.ones((16, 2 * BLK), BF16)

    def gather_values(i, w_ref, f_ref):
        _, qd, b1, b2, _, _, _, _ = fields(items_ref, i)
        for p in range(2):
            r = slice(64 * p, 64 * p + 64)
            lhs = jnp.concatenate([vt_ref[b1, r, :], vt_ref[b2, r, :]], axis=1)
            lhs = jnp.concatenate([lhs, ones], axis=0)
            o = jnp.dot(lhs, w_ref[:, 256 * p : 256 * p + 256], preferred_element_type=F32)
            for k in range(2):
                h = 2 * p + k
                c = slice(BLK * k, BLK * k + BLK)
                fac = f_ref[h : h + 1, :]
                a = slice(h * HEAD, (h + 1) * HEAD)
                acc_ref[qd, a, :] = acc_ref[qd, a, :] * fac + o[k * HEAD : (k + 1) * HEAD, c]
                l_ref[qd, h : h + 1, :] = l_ref[qd, h : h + 1, :] * fac + o[64:65, c]

    def weigh(i, s_ref, x_ref, w_ref, f_ref):
        _, qd, _, _, _, _, _, _ = fields(items_ref, i)
        for h in range(HEADS):
            c = slice(BLK * h, BLK * h + BLK)
            old = m_ref[qd, h : h + 1, :]
            new = jnp.maximum(old, x_ref[h : h + 1, :])
            f_ref[h : h + 1, :] = jnp.exp2(old - new)
            m_ref[qd, h : h + 1, :] = new
            w_ref[:, c] = jnp.exp2(s_ref[:, c] - new).astype(BF16)

    def score(i, s_ref, x_ref):
        q, _, b1, b2, w1, w2, live1, live2 = fields(items_ref, i)
        kk = jnp.concatenate([k_ref[b1], k_ref[b2]], axis=0)
        words = [words_ref[w1] * live1, words_ref[w2] * live2]
        for p in range(2):
            s = jnp.dot(kk, qbd_ref[q, :, 256 * p : 256 * p + 256], preferred_element_type=F32)
            peak = [None, None]
            for g in range(32):
                row = words[g // 16][g % 16 : g % 16 + 1, :]
                hit = (jnp.broadcast_to(row, (8, BLK)) & bit) != 0
                for k in range(2):
                    v = jnp.where(hit, s[8 * g : 8 * g + 8, BLK * k : BLK * k + BLK] * SCALE, NEG)
                    s_ref[8 * g : 8 * g + 8, 256 * p + BLK * k : 256 * p + BLK * k + BLK] = v
                    peak[k] = v if peak[k] is None else jnp.maximum(peak[k], v)
            for k in range(2):
                x_ref[2 * p + k : 2 * p + k + 1, :] = jnp.max(peak[k], axis=0, keepdims=True)

    def body(j, carry):
        for e in range(2):
            i = 2 * j + e
            score(i + 2, s_refs[e], x_refs[e])
            gather_values(i, w_refs[e], f_refs[e])
            weigh(i + 1, s_refs[1 - e], x_refs[1 - e], w_refs[1 - e], f_refs[1 - e])
        return carry

    lax.fori_loop(0, lax.shift_right_logical(count + 3, 1), body, 0)


def phase_kernel(phase, n_chunks, items_ref, count_ref, bounded_ref, words_ref, qbd_ref, qnorm_ref, wk_ref, wvt_ref, *refs):
    first, last = phase == 0, phase == 2
    chunks, refs = refs[:n_chunks], refs[n_chunks:]
    if not first:
        refs = refs[3:]
    m_ref, l_ref, acc_ref, out_ref = refs[:4]
    k_ref, vt_ref, norm_ref = refs[4:7]
    s_refs, x_refs, w_refs, f_refs = refs[7:9], refs[9:11], refs[11:13], refs[13:15]
    items_ref = items_ref.at[phase]
    if first:
        m_ref[...] = jnp.full_like(m_ref, NEG)
        l_ref[...] = jnp.zeros_like(l_ref)
        acc_ref[...] = jnp.zeros_like(acc_ref)
    project(chunks, wk_ref, wvt_ref, k_ref, vt_ref, norm_ref)
    before = bounded_ref[0] == 1
    fits = jnp.max(norm_ref[...]) * jnp.max(qnorm_ref[...]) * 1.02 * SCALE * SCALE <= LIMIT * LIMIT
    bounded = jnp.logical_and(before, fits)
    count = count_ref[phase]

    @pl.when(bounded)
    def _():
        visit_bounded(items_ref, count, words_ref, qbd_ref, k_ref, vt_ref, l_ref, acc_ref, w_refs)

    @pl.when(jnp.logical_not(bounded))
    def _():
        @pl.when(before)
        def _():
            m_ref[...] = jnp.where(l_ref[...] > 0, 0.0, NEG)

        visit(items_ref, count, words_ref, qbd_ref, k_ref, vt_ref, m_ref, l_ref, acc_ref, s_refs, x_refs, w_refs, f_refs)

    if last:
        def emit(q, carry):
            tot = l_ref[q, :HEADS, :]
            for h in range(HEADS):
                a = slice(h * HEAD, (h + 1) * HEAD)
                out_ref[q, a, :] = (acc_ref[q, a, :] / tot[h : h + 1, :]).astype(BF16)
            top = jnp.where(bounded, jnp.floor(jnp.log2(tot)), m_ref[q, :HEADS, :])
            high = top.astype(BF16).astype(F32)
            low = (top - high).astype(BF16).astype(F32)
            base = jnp.where(bounded, 0.0, top)
            mass = tot * jnp.exp2(base - high - low)
            mass_high = mass.astype(BF16).astype(F32)
            parts = [high, low, mass_high, mass - mass_high]
            out_ref[q, BLK:, :] = jnp.concatenate(parts, axis=0).astype(BF16)
            return carry

        lax.fori_loop(0, DESTS, emit, 0, unroll=4)
    else:
        out_ref[0] = bounded.astype(jnp.int32)


def run_phase(phase, items, count, words, qbd, qnorm, wk, wvt, chunks, state):
    first, last = phase == 0, phase == 2
    blocks = sum(c.shape[0] for c in chunks) // BLK
    out_shape = (
        jax.ShapeDtypeStruct((DESTS + 1, 8, BLK), F32),
        jax.ShapeDtypeStruct((DESTS + 1, 8, BLK), F32),
        jax.ShapeDtypeStruct((DESTS + 1, BLK, BLK), F32),
        jax.ShapeDtypeStruct((DESTS, MSG, BLK), BF16) if last else jax.ShapeDtypeStruct((1,), jnp.int32),
    )
    if first:
        state = (jnp.ones((1,), jnp.int32),)
    ins = (items, count, state[-1], words, qbd, qnorm, wk, wvt, *chunks, *state[:-1])
    specs = [smem()] * 3 + [vmem()] * (len(ins) - 3)
    return pl.pallas_call(
        functools.partial(phase_kernel, phase, len(chunks)),
        out_shape=out_shape,
        in_specs=specs,
        out_specs=(vmem(), vmem(), vmem(), vmem() if last else smem()),
        input_output_aliases={} if first else {len(ins) - 3 + i: i for i in range(3)},
        scratch_shapes=[
            pltpu.VMEM((blocks, BLK, BLK), BF16),
            pltpu.VMEM((blocks, BLK, BLK), BF16),
            pltpu.VMEM((8, BLK), F32),
            pltpu.VMEM((2 * BLK, HEADS * BLK), F32),
            pltpu.VMEM((2 * BLK, HEADS * BLK), F32),
            pltpu.VMEM((8, BLK), F32),
            pltpu.VMEM((8, BLK), F32),
            pltpu.VMEM((2 * BLK, HEADS * BLK), BF16),
            pltpu.VMEM((2 * BLK, HEADS * BLK), BF16),
            pltpu.VMEM((8, BLK), F32),
            pltpu.VMEM((8, BLK), F32),
        ],
        compiler_params=pltpu.CompilerParams(vmem_limit_bytes=24 * 1024 * 1024),
        cost_estimate=pl.CostEstimate(flops=500_000_000, bytes_accessed=8_000_000, transcendentals=4_000_000),
    )(*ins)


def combine_kernel(msg_ref, wo_ref, out_ref):
    sources = msg_ref.shape[0]
    for b in range(2):
        stats = []
        for j in range(sources):
            st = msg_ref[j, b, BLK:, :].astype(F32)
            stats.append((st[0:4] + st[4:8], st[8:12] + st[12:16]))
        peak = functools.reduce(jnp.maximum, [s[0] for s in stats])
        mass = [tot * jnp.exp2(top - peak) for top, tot in stats]
        denom = functools.reduce(jnp.add, mass)
        rows = []
        for h in range(HEADS):
            a = slice(h * HEAD, (h + 1) * HEAD)
            num = functools.reduce(
                jnp.add,
                [msg_ref[j, b, a, :].astype(F32) * mass[j][h : h + 1, :] for j in range(sources)],
            )
            rows.append(num / denom[h : h + 1, :])
        att = jnp.concatenate(rows, axis=0).astype(BF16)
        mixed = lax.dot_general(att, wo_ref[...], TN, preferred_element_type=F32)
        out_ref[b * BLK : (b + 1) * BLK, :] = mixed.astype(BF16)


def make_items(lists, counts, my_dst):
    my_x = my_dst // 8
    owner = lists // 2
    dx = (owner // 8 - my_x) % 4
    chunk = jnp.where(dx == 1, 1, 0)
    pos = (chunk * 8 + owner % 8) * 2 + lists % 2
    phase = jnp.where(dx == 0, 0, jnp.where(dx == 2, 2, 1))
    slots = jnp.arange(SLOTS, dtype=jnp.int32)
    dests = jnp.arange(DESTS, dtype=jnp.int32)
    word = dests[:, None] * SLOTS + slots[None, :]
    live = slots[None, :] < counts[:, None]
    pay = word | (pos << 8) | (1 << 16)
    sel = live[None] & (phase[None] == jnp.arange(3, dtype=jnp.int32)[:, None, None])
    sel_i = sel.astype(jnp.int32)
    before = (slots[None, :] < slots[:, None]).astype(jnp.int32)
    rank = jnp.sum(sel_i[:, :, None, :] * before[None, None], axis=-1)
    per_dest = (jnp.sum(sel_i, axis=-1) + 1) // 2
    offset = jnp.sum(per_dest[:, None, :] * before[None], axis=-1)
    total = jnp.sum(per_dest, axis=-1)
    item = jnp.where(sel, offset[:, :, None] + rank // 2 + 2, -1)
    key = (item * 2 + rank % 2).reshape(3, 1, DESTS * SLOTS)
    want = jnp.arange(2 * ITEMS, dtype=jnp.int32)
    want = (want % ITEMS) * 2 + want // ITEMS
    table = jnp.sum(jnp.where(key == want[None, :, None], pay.reshape(1, 1, -1), 0), axis=-1)
    return table.reshape(3, 2, ITEMS), total


def x_step(rows, step):
    return lax.ppermute(rows, "dst", [(x * 8 + z, ((x + step) % 4) * 8 + z) for x in range(4) for z in range(8)])


def shards(node_feats, w_query, w_key, w_value, w_out, src_blocks, live_counts, edge_bits):
    own = node_feats[0, 0]
    columns = [[x * 8 + z for z in range(8)] for x in range(4)]
    copies = pl.pallas_call(
        copy_kernel,
        out_shape=jax.ShapeDtypeStruct((8, 2 * BLK, BLK), BF16),
        in_specs=[vmem()],
        out_specs=vmem(),
    )(own)
    base = lax.all_to_all(copies, "dst", 0, 0, axis_index_groups=columns, tiled=True)
    base = base.reshape(16 * BLK, BLK)
    sent, _ = lax.optimization_barrier((own, copies))
    dest_rows = [own] + [lax.ppermute(sent, "src", [(i, (i + s) % 8) for i in range(8)]) for s in range(1, 8)]
    items, total = make_items(src_blocks[0, 0], live_counts[0, 0], lax.axis_index("dst"))
    words = edge_bits[0, 0].reshape(DESTS * SLOTS, 16, BLK)
    qbd, wvt, qnorm = pl.pallas_call(
        prep_kernel,
        out_shape=(
            jax.ShapeDtypeStruct((DESTS, BLK, HEADS * BLK), BF16),
            jax.ShapeDtypeStruct((BLK, BLK), BF16),
            jax.ShapeDtypeStruct((HEADS, 2 * BLK), F32),
        ),
        in_specs=[smem()] + [vmem()] * 10,
        out_specs=(vmem(), vmem(), vmem()),
        compiler_params=pltpu.CompilerParams(vmem_limit_bytes=16 * 1024 * 1024),
    )(lax.axis_index("src").reshape(1), *dest_rows, w_query, w_value)
    base, qnorm, items, total = lax.optimization_barrier((base, qnorm, items, total))
    left = x_step(base, 1)
    right = x_step(base, -1)
    run = functools.partial(run_phase, words=words, qbd=qbd, qnorm=qnorm, wk=w_key, wvt=wvt)
    state = run(0, items, total, chunks=[base], state=None)
    late, left, right, *state = lax.optimization_barrier((base, left, right, *state))
    far = x_step(late, 2)
    state = run(1, items, total, chunks=[left, right], state=state)
    msg = run(2, items, total, chunks=[far], state=state)
    got = lax.all_to_all(msg[3].reshape(8, 2, MSG, BLK), "src", 0, 0, tiled=True)
    mixed = pl.pallas_call(
        combine_kernel,
        out_shape=jax.ShapeDtypeStruct((2 * BLK, BLK), BF16),
        in_specs=[vmem(), vmem()],
        out_specs=vmem(),
    )(got, w_out)
    return mixed.reshape(1, 1, 2 * BLK, BLK)


def solution(mesh):
    in_specs = (
        P("src", "dst", None, None),
        P(),
        P(),
        P(),
        P(),
        P("src", "dst", None, None),
        P("src", "dst", None),
        P("src", "dst", None, None, None, None),
    )
    out_specs = P("src", "dst", None, None)
    return jax.shard_map(shards, mesh=mesh, in_specs=in_specs, out_specs=out_specs, check_vma=False)
```

time: 127 us -> 86.4 us (0.68)
  the two profiles are of different devices: /device:TPU:96 before, /device:TPU:6 now
where the time goes in v2:
time: 86.4 us; the launch traced here: 86.7 us
  blocking collectives  23.6 us (27%)
  starting transfers between devices  21.2 us (25%)
  waiting for transfers between devices  19.6 us (23%)
  Pallas kernels  16.5 us (19%)
  local copies, waits for them, and re-layouts  3.77 us (4%)
  other arithmetic  1.87 us (2%)
    all_to_all x1, blocking collectives, shards(): lax.all_to_all(msg[3].reshape(8, 2, MSG, BLK), 'src', 0, 0, tiled=True)  23.6 us
    ppermute x3, waiting for transfers between devices, x_step(): lax.ppermute(rows, 'dst', [(x * 8 + z, (x + step) % 4 * 8 + z) for x in r...  14.6 us
    pallas_call x3, Pallas kernels, run_phase(): pl.pallas_call(functools.partial(phase_kernel, phase, len(chunks)), out_s...  12.2 us
    all_to_all x1, starting transfers between devices, shards(): lax.all_to_all(copies, 'dst', 0, 0, axis_index_groups=columns, tiled=True)  8.6 us
    ppermute x7, starting transfers between devices, shards(): lax.ppermute(sent, 'src', [(i, (i + s) % 8) for i in range(8)])  7.91 us
    ppermute x7, waiting for transfers between devices, shards(): lax.ppermute(sent, 'src', [(i, (i + s) % 8) for i in range(8)])  4.77 us
    ppermute x3, starting transfers between devices, x_step(): lax.ppermute(rows, 'dst', [(x * 8 + z, (x + step) % 4 * 8 + z) for x in r...  4.7 us
    unnamed x18, local copies, waits for them, and re-layouts  2.95 us
  transfers between devices with their start and end apart: 11, of which 6 were waited for; matrix products, arithmetic and copies ran while one was open for 3% of the time, Pallas kernels for 10%

profile of v2, /device:TPU:6, one launch (start us, length us, event | category | flops | bytes accessed | tf_op | source)
XLA Modules:
  0.0 86.7 jit_solution(12803831647687328782)
XLA Ops:
  0.0 1.9 %shard_map.82 = bf16[8,256,128]{2,1,0:T(8,128)(2,1)} custom-call(bf16[256,128]{1,0:T(8,128)(2,1)} %bitcast.34), custom_call_target="tpu_custom_call" | custom-call | tf_op jit(solution)/shard_map/pallas_call | solution.py:351
  1.9 8.6 %all-to-all-start = ((bf16[8,256,128]{2,1,0:T(8,128)(2,1)}), bf16[8,256,128]{2,1,0:T(8,128)(2,1)S(1)}, u32[]{:S(2)}, u32[]{:S(2)}) async-start(bf16[8,256,128]{2,1,0:T(8,128)(2,1)} %shard_map.82), calls=%async_computation | async-start | bytes 1048576 | tf_op jit(solution)/shard_map/all_to_all | solution.py:357
  10.5 2.2 %collective-permute-start.6 = (bf16[256,128]{1,0:T(8,128)(2,1)S(1)}, bf16[256,128]{1,0:T(8,128)(2,1)S(1)}, u32[]{:S(2)}, u32[]{:S(2)}) collective-permute-start(bf16[256,128]{1,0:T(8,128)(2,1)S(1)} %bitcast.35), channel_id=1, source_target_pairs={{0,7},{1,0},{2,1},{3,2},{4,3},{5,4},{6,5},{7,6},{8,15},{9,8},{10,9... | collective-permute-start | bytes 196616 | tf_op jit(solution)/shard_map/ppermute | solution.py:360
  12.7 0.9 %collective-permute-start.5 = (bf16[256,128]{1,0:T(8,128)(2,1)S(1)}, bf16[256,128]{1,0:T(8,128)(2,1)S(1)}, u32[]{:S(2)}, u32[]{:S(2)}) collective-permute-start(bf16[256,128]{1,0:T(8,128)(2,1)S(1)} %bitcast.36), channel_id=1, source_target_pairs={{0,6},{1,7},{2,0},{3,1},{4,2},{5,3},{6,4},{7,5},{8,14},{9,15},{10,... | collective-permute-start | bytes 196616 | tf_op jit(solution)/shard_map/ppermute | solution.py:360
  14.0 2.9 %collective-permute-start.3 = (bf16[256,128]{1,0:T(8,128)(2,1)S(1)}, bf16[256,128]{1,0:T(8,128)(2,1)S(1)}, u32[]{:S(2)}, u32[]{:S(2)}) collective-permute-start(bf16[256,128]{1,0:T(8,128)(2,1)S(1)} %bitcast.38), channel_id=1, source_target_pairs={{0,4},{1,5},{2,6},{3,7},{4,0},{5,1},{6,2},{7,3},{8,12},{9,13},{10,... | collective-permute-start | bytes 196616 | tf_op jit(solution)/shard_map/ppermute | solution.py:360
  18.0 0.9 %multiply_reduce_fusion = s32[3,16,16]{2,1,0:T(8,128)S(1)} fusion(s32[16,16]{1,0:T(8,128)S(1)} %fusion.8, s32[3,16,16]{2,1,0:T(8,128)S(1)} %fusion.1), kind=kLoop, calls=%fused_computation.1 | loop fusion | flops 23808 | bytes 7168 | tf_op jit(solution)/shard_map/reduce_sum | solution.py:332
  19.3 0.5 collective-permute-start.1
  19.7 1.1 %collective-permute-start = (bf16[256,128]{1,0:T(8,128)(2,1)S(1)}, bf16[256,128]{1,0:T(8,128)(2,1)S(1)}, u32[]{:S(2)}, u32[]{:S(2)}) collective-permute-start(bf16[256,128]{1,0:T(8,128)(2,1)S(1)} %bitcast.41), channel_id=1, source_target_pairs={{0,1},{1,2},{2,3},{3,4},{4,5},{5,6},{6,7},{7,0},{8,9},{9,10},{10,1... | collective-permute-start | bytes 196616 | tf_op jit(solution)/shard_map/ppermute | solution.py:360
  21.2 1.0 %collective-permute-done.2.refs_3_ = bf16[256,128]{1,0:T(8,128)(2,1)S(1)} collective-permute-done((bf16[256,128]{1,0:T(8,128)(2,1)S(1)}, bf16[256,128]{1,0:T(8,128)(2,1)S(1)}, u32[]{:S(2)}, u32[]{:S(2)}) %collective-permute-start.2) | collective-permute-done | bytes 65568 | tf_op jit(solution)/shard_map/ppermute | solution.py:360
  22.2 3.3 %collective-permute-done.1.refs_2_ = bf16[256,128]{1,0:T(8,128)(2,1)S(1)} collective-permute-done((bf16[256,128]{1,0:T(8,128)(2,1)S(1)}, bf16[256,128]{1,0:T(8,128)(2,1)S(1)}, u32[]{:S(2)}, u32[]{:S(2)}) %collective-permute-start.1) | collective-permute-done | bytes 65568 | tf_op jit(solution)/shard_map/ppermute | solution.py:360
  25.5 0.5 collective-permute-done.refs_1_
  26.0 0.4 shard_map.83
  26.4 1.3 %copy-done.4 = bf16[16,128,512]{2,1,0:T(8,128)(2,1)} copy-done((bf16[16,128,512]{2,1,0:T(8,128)(2,1)}, bf16[16,128,512]{2,1,0:T(8,128)(2,1)S(1)}, u32[]{:S(2)}) %copy-start.4) | copy-done | bytes 2097176
  28.0 0.8 collective-permute-start.8
  28.8 2.4 %collective-permute-start.7 = (bf16[2048,128]{1,0:T(8,128)(2,1)S(1)}, bf16[2048,128]{1,0:T(8,128)(2,1)S(1)}, u32[]{:S(2)}, u32[]{:S(2)}) collective-permute-start(bf16[2048,128]{1,0:T(8,128)(2,1)S(1)} %bitcast.31), channel_id=1, source_target_pairs={{0,64},{8,72},{16,80},{24,88},{32,96},{40,104},{48,112},{56,120},{... | collective-permute-start | bytes 1572872 | tf_op jit(solution)/shard_map/ppermute | solution.py:345
  31.2 1.6 %copy-done.5 = bf16[16,128,512]{2,1,0:T(8,128)(2,1)S(1)} copy-done((bf16[16,128,512]{2,1,0:T(8,128)(2,1)S(1)}, bf16[16,128,512]{2,1,0:T(8,128)(2,1)}, u32[]{:S(2)}) %copy-start.5) | copy-done | bytes 2097176
  32.8 3.6 %shard_map.84 = (f32[17,8,128]{2,1,0:T(8,128)S(1)}, f32[17,8,128]{2,1,0:T(8,128)S(1)}, f32[17,128,128]{2,1,0:T(8,128)S(1)}, s32[1]{0:T(128)}) custom-call(s32[3,2,144]{2,1,0:T(2,128)S(1)} %reshape.367.items_ref, s32[3]{0:T(128)S(1)} %get-tuple-element.32.count_ref, s32[1]{0:T(128)} %constant.134.clone.1.bounded_ref, s32[256,16,128]{2,1,0:T(8,128)S(1)} %bitcast.43, ...), custom_call_target="tpu_custom_call" | custom-call | flops 500000000 | bytes 8000000 | tf_op jit(solution)/shard_map/pallas_call | solution.py:270
  36.4 6.6 %collective-permute-done.8.refs_1_ = bf16[2048,128]{1,0:T(8,128)(2,1)S(1)} collective-permute-done((bf16[2048,128]{1,0:T(8,128)(2,1)S(1)}, bf16[2048,128]{1,0:T(8,128)(2,1)S(1)}, u32[]{:S(2)}, u32[]{:S(2)}) %collective-permute-start.8) | collective-permute-done | bytes 524320 | tf_op jit(solution)/shard_map/ppermute | solution.py:345
  43.1 1.5 %collective-permute-start.9 = (bf16[2048,128]{1,0:T(8,128)(2,1)S(1)}, bf16[2048,128]{1,0:T(8,128)(2,1)S(1)}, u32[]{:S(2)}, u32[]{:S(2)}) collective-permute-start(bf16[2048,128]{1,0:T(8,128)(2,1)S(1)} %bitcast.33), channel_id=1, source_target_pairs={{0,128},{8,136},{16,144},{24,152},{32,160},{40,168},{48,176},{56,1... | collective-permute-start | bytes 1572872 | tf_op jit(solution)/shard_map/ppermute | solution.py:345
  44.5 5.1 %shard_map.85 = (f32[17,8,128]{2,1,0:T(8,128)S(1)}, f32[17,8,128]{2,1,0:T(8,128)S(1)}, f32[17,128,128]{2,1,0:T(8,128)S(1)}, s32[1]{0:T(128)}) custom-call(s32[3,2,144]{2,1,0:T(2,128)S(1)} %reshape.367.items_ref, s32[3]{0:T(128)S(1)} %get-tuple-element.32.count_ref, ...), custom_call_target="tpu_custom_call", output_to_operand_aliasing={{0}: (10, {}), {1}: (11, {}), {2}: (12, {})} | custom-call | flops 500000000 | bytes 8000000 | tf_op jit(solution)/shard_map/pallas_call | solution.py:270
  49.6 8.0 %collective-permute-done.9.refs_0_ = bf16[2048,128]{1,0:T(8,128)(2,1)S(1)} collective-permute-done((bf16[2048,128]{1,0:T(8,128)(2,1)S(1)}, bf16[2048,128]{1,0:T(8,128)(2,1)S(1)}, u32[]{:S(2)}, u32[]{:S(2)}) %collective-permute-start.9) | collective-permute-done | bytes 524320 | tf_op jit(solution)/shard_map/ppermute | solution.py:345
  57.6 3.5 %shard_map.86 = (f32[17,8,128]{2,1,0:T(8,128)S(1)}, f32[17,8,128]{2,1,0:T(8,128)S(1)}, f32[17,128,128]{2,1,0:T(8,128)S(1)}, bf16[16,144,128]{2,1,0:T(8,128)(2,1)S(1)}) custom-call(s32[3,2,144]{2,1,0:T(2,128)S(1)} %reshape.367.items_ref, s32[3]{0:T(128)S(1)} %get-tuple-element.32.count_ref, ...), custom_call_target="tpu_custom_call", output_to_operand_aliasing={{0}: (9, {}), {1}: (10, {}), {2}: (11, {})} | custom-call | flops 500000000 | bytes 8000000 | tf_op jit(solution)/shard_map/pallas_call | solution.py:270
  61.1 23.6 %all_to_all.10.msg_ref = bf16[8,2,144,128]{3,2,1,0:T(8,128)(2,1)} all-to-all(bf16[8,2,144,128]{3,2,1,0:T(8,128)(2,1)S(1)} %bitcast.29), channel_id=1, replica_groups=mesh['dst'=32,'src'=8] {'src'}, dimensions={0} | all-to-all | bytes 1179648 | tf_op jit(solution)/shard_map/all_to_all | solution.py:383
  84.6 2.0 %shard_map.87 = bf16[256,128]{1,0:T(8,128)(2,1)} custom-call(bf16[8,2,144,128]{3,2,1,0:T(8,128)(2,1)} %all_to_all.10.msg_ref, bf16[128,128]{1,0:T(8,128)(2,1)} %wo_ref.1), custom_call_target="tpu_custom_call" | custom-call | tf_op jit(solution)/shard_map/pallas_call | solution.py:384
  (49 shorter events, 2.5 us)
Async XLA Ops:
  0.0 10.5 %copy-start = (bf16[1,1,256,128]{3,2,1,0:T(8,128)(2,1)S(1)}, bf16[1,1,256,128]{3,2,1,0:T(8,128)(2,1)}, u32[]{:S(2)}) copy-start(bf16[1,1,256,128]{3,2,1,0:T(8,128)(2,1)} %param.8) | copy-start | bytes 196612
  0.0 16.9 %copy-start.8 = (s32[1,1,16]{2,1,0:T(1,128)S(1)}, s32[1,1,16]{2,1,0:T(1,128)}, u32[]{:S(2)}) copy-start(s32[1,1,16]{2,1,0:T(1,128)} %param.14) | copy-start | bytes 196
  0.0 17.1 %copy-start.7 = (s32[1,1,16,16]{3,2,1,0:T(8,128)S(1)}, s32[1,1,16,16]{3,2,1,0:T(8,128)}, u32[]{:S(2)}) copy-start(s32[1,1,16,16]{3,2,1,0:T(8,128)} %param.13) | copy-start | bytes 3076
  0.0 26.0 %copy-start.2 = (bf16[128,128]{1,0:T(8,128)(2,1)S(1)}, bf16[128,128]{1,0:T(8,128)(2,1)}, u32[]{:S(2)}) copy-start(bf16[128,128]{1,0:T(8,128)(2,1)} %refs_9_.1) | copy-start | bytes 98308
  0.0 26.0 %copy-start.1 = (bf16[128,128]{1,0:T(8,128)(2,1)S(1)}, bf16[128,128]{1,0:T(8,128)(2,1)}, u32[]{:S(2)}) copy-start(bf16[128,128]{1,0:T(8,128)(2,1)} %refs_8_.1) | copy-start | bytes 98308
  0.0 31.2 %copy-start.3 = (s32[1,1,16,16,16,128]{5,4,3,2,1,0:T(8,128)S(1)}, s32[1,1,16,16,16,128]{5,4,3,2,1,0:T(8,128)}, u32[]{:S(2)}) copy-start(s32[1,1,16,16,16,128]{5,4,3,2,1,0:T(8,128)} %param.15) | copy-start | bytes 6291460
  1.9 29.3 %copy-start.6 = (bf16[128,128]{1,0:T(8,128)(2,1)S(1)}, bf16[128,128]{1,0:T(8,128)(2,1)}, u32[]{:S(2)}) copy-start(bf16[128,128]{1,0:T(8,128)(2,1)} %wk_ref.5) | copy-start | bytes 98308
  1.9 26.1 %all-to-all-start = ((bf16[8,256,128]{2,1,0:T(8,128)(2,1)}), bf16[8,256,128]{2,1,0:T(8,128)(2,1)S(1)}, u32[]{:S(2)}, u32[]{:S(2)}) async-start(bf16[8,256,128]{2,1,0:T(8,128)(2,1)} %shard_map.82), calls=%async_computation | async-start | bytes 1048576 | tf_op jit(solution)/shard_map/all_to_all | solution.py:357
  10.5 8.7 %collective-permute-start.6 = (bf16[256,128]{1,0:T(8,128)(2,1)S(1)}, bf16[256,128]{1,0:T(8,128)(2,1)S(1)}, u32[]{:S(2)}, u32[]{:S(2)}) collective-permute-start(bf16[256,128]{1,0:T(8,128)(2,1)S(1)} %bitcast.35), channel_id=1, source_target_pairs={{0,7},{1,0},{2,1},{3,2},{4,3},{5,4},{6,5},{7,6},{8,15},{9,8},{10,9... | collective-permute-start | bytes 196616 | tf_op jit(solution)/shard_map/ppermute | solution.py:360
  12.7 7.0 %collective-permute-start.5 = (bf16[256,128]{1,0:T(8,128)(2,1)S(1)}, bf16[256,128]{1,0:T(8,128)(2,1)S(1)}, u32[]{:S(2)}, u32[]{:S(2)}) collective-permute-start(bf16[256,128]{1,0:T(8,128)(2,1)S(1)} %bitcast.36), channel_id=1, source_target_pairs={{0,6},{1,7},{2,0},{3,1},{4,2},{5,3},{6,4},{7,5},{8,14},{9,15},{10,... | collective-permute-start | bytes 196616 | tf_op jit(solution)/shard_map/ppermute | solution.py:360
  13.6 7.6 %collective-permute-start.4 = (bf16[256,128]{1,0:T(8,128)(2,1)S(1)}, bf16[256,128]{1,0:T(8,128)(2,1)S(1)}, u32[]{:S(2)}, u32[]{:S(2)}) collective-permute-start(bf16[256,128]{1,0:T(8,128)(2,1)S(1)} %bitcast.37), channel_id=1, source_target_pairs={{0,5},{1,6},{2,7},{3,0},{4,1},{5,2},{6,3},{7,4},{8,13},{9,14},{10,... | collective-permute-start | bytes 196616 | tf_op jit(solution)/shard_map/ppermute | solution.py:360
  14.0 7.2 %collective-permute-start.3 = (bf16[256,128]{1,0:T(8,128)(2,1)S(1)}, bf16[256,128]{1,0:T(8,128)(2,1)S(1)}, u32[]{:S(2)}, u32[]{:S(2)}) collective-permute-start(bf16[256,128]{1,0:T(8,128)(2,1)S(1)} %bitcast.38), channel_id=1, source_target_pairs={{0,4},{1,5},{2,6},{3,7},{4,0},{5,1},{6,2},{7,3},{8,12},{9,13},{10,... | collective-permute-start | bytes 196616 | tf_op jit(solution)/shard_map/ppermute | solution.py:360
  16.9 5.3 %collective-permute-start.2 = (bf16[256,128]{1,0:T(8,128)(2,1)S(1)}, bf16[256,128]{1,0:T(8,128)(2,1)S(1)}, u32[]{:S(2)}, u32[]{:S(2)}) collective-permute-start(bf16[256,128]{1,0:T(8,128)(2,1)S(1)} %bitcast.39), channel_id=1, source_target_pairs={{0,3},{1,4},{2,5},{3,6},{4,7},{5,0},{6,1},{7,2},{8,11},{9,12},{10,... | collective-permute-start | bytes 196616 | tf_op jit(solution)/shard_map/ppermute | solution.py:360
  19.3 6.3 %collective-permute-start.1 = (bf16[256,128]{1,0:T(8,128)(2,1)S(1)}, bf16[256,128]{1,0:T(8,128)(2,1)S(1)}, u32[]{:S(2)}, u32[]{:S(2)}) collective-permute-start(bf16[256,128]{1,0:T(8,128)(2,1)S(1)} %bitcast.40), channel_id=1, source_target_pairs={{0,2},{1,3},{2,4},{3,5},{4,6},{5,7},{6,0},{7,1},{8,10},{9,11},{10,... | collective-permute-start | bytes 196616 | tf_op jit(solution)/shard_map/ppermute | solution.py:360
  19.7 6.3 %collective-permute-start = (bf16[256,128]{1,0:T(8,128)(2,1)S(1)}, bf16[256,128]{1,0:T(8,128)(2,1)S(1)}, u32[]{:S(2)}, u32[]{:S(2)}) collective-permute-start(bf16[256,128]{1,0:T(8,128)(2,1)S(1)} %bitcast.41), channel_id=1, source_target_pairs={{0,1},{1,2},{2,3},{3,4},{4,5},{5,6},{6,7},{7,0},{8,9},{9,10},{10,1... | collective-permute-start | bytes 196616 | tf_op jit(solution)/shard_map/ppermute | solution.py:360
  26.4 1.3 %copy-start.4 = (bf16[16,128,512]{2,1,0:T(8,128)(2,1)}, bf16[16,128,512]{2,1,0:T(8,128)(2,1)S(1)}, u32[]{:S(2)}) copy-start(bf16[16,128,512]{2,1,0:T(8,128)(2,1)S(1)} %get-tuple-element.34.qbd_ref) | copy-start | bytes 6291460
  28.0 15.1 %collective-permute-start.8 = (bf16[2048,128]{1,0:T(8,128)(2,1)S(1)}, bf16[2048,128]{1,0:T(8,128)(2,1)S(1)}, u32[]{:S(2)}, u32[]{:S(2)}) collective-permute-start(bf16[2048,128]{1,0:T(8,128)(2,1)S(1)} %bitcast.30), channel_id=1, source_target_pairs={{0,192},{8,200},{16,208},{24,216},{32,224},{40,232},{48,240},{56,2... | collective-permute-start | bytes 1572872 | tf_op jit(solution)/shard_map/ppermute | solution.py:345
  28.8 14.2 %collective-permute-start.7 = (bf16[2048,128]{1,0:T(8,128)(2,1)S(1)}, bf16[2048,128]{1,0:T(8,128)(2,1)S(1)}, u32[]{:S(2)}, u32[]{:S(2)}) collective-permute-start(bf16[2048,128]{1,0:T(8,128)(2,1)S(1)} %bitcast.31), channel_id=1, source_target_pairs={{0,64},{8,72},{16,80},{24,88},{32,96},{40,104},{48,112},{56,120},{... | collective-permute-start | bytes 1572872 | tf_op jit(solution)/shard_map/ppermute | solution.py:345
  31.2 1.6 %copy-start.5 = (bf16[16,128,512]{2,1,0:T(8,128)(2,1)S(1)}, bf16[16,128,512]{2,1,0:T(8,128)(2,1)}, u32[]{:S(2)}) copy-start(bf16[16,128,512]{2,1,0:T(8,128)(2,1)} %copy-done.4) | copy-start | bytes 6291460
  43.1 14.5 %collective-permute-start.9 = (bf16[2048,128]{1,0:T(8,128)(2,1)S(1)}, bf16[2048,128]{1,0:T(8,128)(2,1)S(1)}, u32[]{:S(2)}, u32[]{:S(2)}) collective-permute-start(bf16[2048,128]{1,0:T(8,128)(2,1)S(1)} %bitcast.33), channel_id=1, source_target_pairs={{0,128},{8,136},{16,144},{24,152},{32,160},{40,168},{48,176},{56,1... | collective-permute-start | bytes 1572872 | tf_op jit(solution)/shard_map/ppermute | solution.py:345
